TPU v7x, 32 devices: a whole 2x2x4 slice. The times are simulated.
32 devices in a mesh: lat: 8 (over z, x), dep: 4 (over y, core).
Axes of the slice: x: 2, y: 2, z: 4, core: 2. Of those that a mesh axis runs over, the one named last changes fastest.
Arguments:
- kernel: bfloat16 [16384, 64, 128], P(('lat', 'dep')), may hold values from -0.1875 to 0.1875
- coefficient: float32 [16384, 256], P(('lat', 'dep')), may hold values from -3 to 3
- observed: float32 [2048, 64], P(('lat', 'dep')), may hold values from -6 to 6
- ray_brick: int32 [16384, 1], P(('lat', 'dep')), may hold values from 0 to 31; in each aligned block of 512 rows (0 to 511, 512 to 1023, ...) at most 24 rows name the same one
- tile_index: int32 [16384], P(('lat', 'dep')), may hold values from 0 to 511
- ray_count: int32 [32], P(('lat', 'dep')), may hold values from 32 to 64, as said below
- earth_model: float32 [32, 4, 512, 128], P(('lat', 'dep')), may hold values from -6 to 6
Outputs:
- residual: float32 [2048, 64], P(('lat', 'dep'))
- gradient: float32 [32, 4, 512, 128], P(('lat', 'dep'))
Inputs may be any that keep to these rules, and one draw needn't show every extreme that they name: `ray_brick`: among the hits of one device no brick is named more than 24 times, a bound that some block reaches. `ray_count`: the largest count is exactly 64.
All inputs are finite; a program needn't handle non-finite values.
Results may differ from a plain program's by a relative error of at most 0.0037.
Values may be sent and summed in bfloat16 or wider, within the bound.
A program may use at most 64 MiB of HBM per device.

v0:
```python
import jax
import jax.numpy as jnp
from jax import lax
from jax.sharding import PartitionSpec as P


def per_device(kernel, coefficient, observed, ray_brick, tile_index, ray_count, earth_model):
    hit_count, band_count, cell_count = kernel.shape
    param_count = earth_model.shape[1]
    tile_count = earth_model.shape[2]
    ray_rows = observed.shape[0]
    per_ray = hit_count // ray_rows
    lat_count = lax.axis_size("lat")
    dep_count = lax.axis_size("dep")
    device_count = lat_count * dep_count
    slot_count = max(2, 3 * hit_count // (2 * device_count))
    slot_total = device_count * slot_count
    target = ray_brick[:, 0]
    live_rays = jnp.arange(ray_rows) < ray_count[0]
    live_hits = jnp.repeat(live_rays, per_ray)
    hit_order = jnp.arange(hit_count)
    earlier = (
        (target[None, :] == target[:, None])
        & (hit_order[None, :] < hit_order[:, None])
        & live_hits[None, :]
    )
    rank_within = jnp.sum(earlier.astype(jnp.int32), axis=1)
    slot_of_hit = jnp.where(live_hits, target * slot_count + rank_within, slot_total)
    wanted = jnp.zeros((slot_total,), jnp.int32).at[slot_of_hit].set(tile_index + 1, mode="drop")
    wanted = wanted.reshape(lat_count, dep_count, slot_count)
    model_low = earth_model[0].astype(jnp.bfloat16)
    requests = lax.all_to_all(
        lax.all_to_all(wanted, "lat", split_axis=0, concat_axis=0, tiled=True),
        "dep",
        split_axis=1,
        concat_axis=1,
        tiled=True,
    )
    lookup = jnp.maximum(requests - 1, 0)
    blocks = jnp.take(model_low, lookup.reshape(-1), axis=1)
    blocks = blocks.reshape(param_count, lat_count, dep_count, slot_count, cell_count)
    arrived = lax.all_to_all(
        lax.all_to_all(blocks, "lat", split_axis=1, concat_axis=1, tiled=True),
        "dep",
        split_axis=2,
        concat_axis=2,
        tiled=True,
    )
    own_blocks = jnp.take(
        arrived.reshape(param_count, slot_total, cell_count),
        jnp.minimum(slot_of_hit, slot_total - 1),
        axis=1,
    )
    coefficient_split = coefficient.reshape(hit_count, param_count, band_count)
    sensitivity = jnp.einsum("hbc,phc->hpb", kernel, own_blocks, preferred_element_type=jnp.float32)
    contribution = jnp.sum(coefficient_split * sensitivity, axis=1)
    predicted = jnp.sum(contribution.reshape(ray_rows, per_ray, band_count), axis=1)
    residual = jnp.where(live_rays[:, None], predicted - observed, jnp.zeros_like(predicted))
    residual_hit = jnp.repeat(residual, per_ray, axis=0)
    weight = (coefficient_split * residual_hit[:, None, :]).astype(jnp.bfloat16)
    gradient_term = jnp.einsum("hpb,hbc->phc", weight, kernel, preferred_element_type=jnp.float32)
    outgoing = (
        jnp.zeros((param_count, slot_total, cell_count), jnp.float32)
        .at[:, slot_of_hit]
        .set(gradient_term, mode="drop")
    )
    outgoing = outgoing.reshape(param_count, lat_count, dep_count, slot_count, cell_count)
    returned = lax.all_to_all(
        lax.all_to_all(outgoing, "lat", split_axis=1, concat_axis=1, tiled=True),
        "dep",
        split_axis=2,
        concat_axis=2,
        tiled=True,
    )
    segment = jnp.where(requests > 0, requests - 1, tile_count)
    brick_sum = jnp.zeros((param_count, tile_count + 1, cell_count), jnp.float32)
    brick_sum = brick_sum.at[:, segment.reshape(-1)].add(
        returned.reshape(param_count, slot_total, cell_count)
    )
    summed = brick_sum[:, :tile_count]
    return (residual, summed.reshape(1, param_count, tile_count, cell_count))


def solution(mesh):
    return jax.shard_map(
        per_device,
        mesh=mesh,
        in_specs=(
            P(("lat", "dep"), None, None),
            P(("lat", "dep"), None),
            P(("lat", "dep"), None),
            P(("lat", "dep"), None),
            P(("lat", "dep")),
            P(("lat", "dep")),
            P(("lat", "dep"), None, None, None),
        ),
        out_specs=(P(("lat", "dep"), None), P(("lat", "dep"), None, None, None)),
        check_vma=False,
    )
```

profile of v0, /device:TPU:0, one launch (start us, length us, event | category | flops | bytes accessed | tf_op | source)
XLA Modules:
  0.0 195.2 jit_solution(5804145044598475307)
XLA Ops:
  1.3 0.1 broadcast_in_dim.58
  1.4 0.1 and.26
  1.5 0.1 reshape.118
  1.6 1.0 convert_reduce_fusion
  2.6 0.7 and_reduce_fusion
  3.3 0.7 broadcast_add_fusion
  4.0 2.4 %scatter_custom_fusion = s32[768]{0:T(1024)S(1)} fusion(s32[512]{0:T(512)S(1)} %bitcast.47, s32[512]{0:T(512)S(1)} %broadcast_add_fusion, s32[]{:T(128)} %constant.16.clone.1), kind=kCustom, calls=%fused_computation.34 | custom fusion | bytes 3076 | tf_op jit(solution)/shard_map/scatter | solution.py:29
  6.5 0.1 reshape.119
  6.5 13.6 %all_to_all.30 = s32[8,4,24]{2,1,0:T(4,128)S(1)} all-to-all(s32[8,4,24]{2,1,0:T(4,128)S(1)} %reshape.119), channel_id=1, replica_groups=mesh['lat'=8,'dep'=4] {'lat'}, dimensions={0} | all-to-all | bytes 6144 | tf_op jit(solution)/shard_map/all_to_all | solution.py:33
  20.2 0.7 reshape.172
  20.8 3.2 %all-to-all-start.1 = ((s32[4,1,192]{2,1,0:T(1,128)}), s32[4,1,192]{2,1,0:T(1,128)S(1)}, u32[]{:S(2)}, u32[]{:S(2)}) async-start(s32[4,1,192]{2,1,0:T(1,128)} %reshape.172), calls=%async_computation.1 | async-start | bytes 8192 | tf_op jit(solution)/shard_map/all_to_all | solution.py:32
  24.1 1.3 convert_element_type.16
  25.4 0.4 copy.78
  25.8 2.0 %all-to-all-done.1 = s32[4,1,192]{2,1,0:T(1,128)S(1)} async-done(((s32[4,1,192]{2,1,0:T(1,128)}), s32[4,1,192]{2,1,0:T(1,128)S(1)}, u32[]{:S(2)}, u32[]{:S(2)}) %all-to-all-start.1) | async-done | bytes 3104 | tf_op jit(solution)/shard_map/all_to_all | solution.py:32
  27.9 0.5 broadcast.120
  28.4 0.7 reduce.6
  29.0 0.1 reshape.173
  29.2 0.1 reshape.120
  29.3 2.8 %gather_fusion = bf16[768,4,128]{2,1,0:T(4,128)(2,1)S(1)} fusion(bf16[4,512,128]{2,0,1:T(4,128)(2,1)S(1)} %bitcast.40, s32[1024]{0:T(1024)S(1)} %pad_clamp_fusion.1), kind=kCustom, calls=%fused_computation | custom fusion | bytes 1575936 | tf_op jit(solution)/shard_map/jit(_take)/gather | solution.py:40
  32.2 1.1 broadcast_select_fusion
  33.3 22.8 %all_to_all.31 = bf16[4,8,4,24,128]{4,0,3,2,1:T(4,128)(2,1)S(1)} all-to-all(bf16[4,8,4,24,128]{4,0,3,2,1:T(4,128)(2,1)S(1)} %broadcast_select_fusion), channel_id=1, replica_groups=mesh['lat'=8,'dep'=4] {'lat'}, dimensions={1} | all-to-all | bytes 1572864 | tf_op jit(solution)/shard_map/all_to_all | solution.py:43
  56.1 0.0 copy-start
  56.1 1.2 copy.65
  57.3 3.5 %all-to-all-start.3 = ((bf16[4,8,4,24,128]{4,0,3,1,2:T(4,128)(2,1)}), bf16[4,8,4,24,128]{4,0,3,1,2:T(4,128)(2,1)S(1)}, u32[]{:S(2)}, u32[]{:S(2)}) async-start(bf16[4,8,4,24,128]{4,0,3,1,2:T(4,128)(2,1)} %copy.65), calls=%async_computation.3 | async-start | bytes 1572864 | tf_op jit(solution)/shard_map/all_to_all | solution.py:42
  60.8 0.0 copy-done
  60.8 0.2 copy.60
  61.0 0.4 copy.67
  61.4 11.0 %all-to-all-done.3 = bf16[4,8,4,24,128]{4,0,3,1,2:T(4,128)(2,1)S(1)} async-done(((bf16[4,8,4,24,128]{4,0,3,1,2:T(4,128)(2,1)}), bf16[4,8,4,24,128]{4,0,3,1,2:T(4,128)(2,1)S(1)}, u32[]{:S(2)}, u32[]{:S(2)}) %all-to-all-start.3) | async-done | bytes 786464 | tf_op jit(solution)/shard_map/all_to_all | solution.py:42
  72.4 0.3 copy.66
  72.7 2.1 %gather_fusion.1 = bf16[512,4,128]{2,1,0:T(4,128)(2,1)S(1)} fusion(bf16[4,768,128]{2,0,1:T(4,128)(2,1)S(1)} %bitcast.42, s32[1024]{0:T(1024)S(1)} %pad_clamp_fusion), kind=kCustom, calls=%fused_computation.1 | custom fusion | bytes 1050624 | tf_op jit(solution)/shard_map/jit(_take)/gather | solution.py:49
  74.8 0.0 copy-start.2
  74.8 7.0 %fusion = f32[512,64]{1,0:T(8,128)S(1)} fusion(f32[512,4,64]{2,1,0:T(4,128)S(1)} %copy.67, bf16[512,64,128]{2,1,0:T(8,128)(2,1)} %param.7, bf16[512,4,128]{2,1,0:T(4,128)(2,1)S(1)} %gather_fusion.1, pred[512]{0:T(512)(128)(4,1)S(1)} %get-tuple-element.16), kind=kOutput, calls=%fused_computation.6 | convolution fusion | flops 34045952 | bytes 9568768 | tf_op jit(solution)/shard_map/hbc,phc->hpb/dot_general | solution.py:55
  81.8 0.1 bitcast_reduce_fusion
  81.9 0.0 copy-done.2
  81.9 0.1 subtract_select_fusion
  81.9 0.0 copy-start.1
  82.0 0.1 copy.69
  82.1 0.1 multiply_convert_fusion
  82.2 0.3 copy.70
  82.5 5.6 %fusion.12 = f32[512,4,128]{2,1,0:T(4,128)S(1)} fusion(bf16[512,4,64]{2,1,0:T(4,128)(2,1)S(1)} %copy.70, bf16[512,64,128]{2,1,0:T(8,128)(2,1)} %param.7), kind=kOutput, calls=%fused_computation.41 | convolution fusion | flops 33554432 | bytes 9699328 | tf_op jit(solution)/shard_map/hpb,hbc->phc/dot_general | solution.py:61
  88.1 0.0 copy-done.1
  88.1 0.2 broadcast_in_dim.67
  88.3 13.7 %scatter_fusion = f32[4,768,128]{2,0,1:T(4,128)S(1)} fusion(f32[4,768,128]{2,0,1:T(4,128)S(1)} %broadcast_in_dim.67, s32[512]{0:T(512)S(1)} %bitcast.48, f32[512,4,128]{2,1,0:T(4,128)S(1)} %fusion.12), kind=kCustom, calls=%fused_computation.3 | custom fusion | bytes 3147776 | tf_op jit(solution)/shard_map/scatter | solution.py:65
  102.0 40.5 %all_to_all.32 = f32[4,8,4,24,128]{4,0,3,2,1:T(4,128)S(1)} all-to-all(f32[4,8,4,24,128]{4,0,3,2,1:T(4,128)S(1)} %bitcast.36), channel_id=1, replica_groups=mesh['lat'=8,'dep'=4] {'lat'}, dimensions={1} | all-to-all | bytes 3145728 | tf_op jit(solution)/shard_map/all_to_all | solution.py:69
  142.5 1.3 copy.71
  143.8 3.6 %all-to-all-start.5 = ((f32[4,8,4,24,128]{4,0,3,1,2:T(4,128)}), f32[4,8,4,24,128]{4,0,3,1,2:T(4,128)S(1)}, u32[]{:S(2)}, u32[]{:S(2)}) async-start(f32[4,8,4,24,128]{4,0,3,1,2:T(4,128)} %copy.71), calls=%async_computation.5 | async-start | bytes 3145728 | tf_op jit(solution)/shard_map/all_to_all | solution.py:68
  147.4 0.1 reshape.123
  147.5 19.9 %all-to-all-done.5 = f32[4,8,4,24,128]{4,0,3,1,2:T(4,128)S(1)} async-done(((f32[4,8,4,24,128]{4,0,3,1,2:T(4,128)}), f32[4,8,4,24,128]{4,0,3,1,2:T(4,128)S(1)}, u32[]{:S(2)}, u32[]{:S(2)}) %all-to-all-start.5) | async-done | bytes 1572896 | tf_op jit(solution)/shard_map/all_to_all | solution.py:68
  167.4 0.2 copy.72
  167.6 1.0 copy.73
  168.7 0.1 broadcast_in_dim.65
  168.8 25.2 %scatter_fusion.1 = f32[4,513,128]{2,0,1:T(4,128)S(1)} fusion(f32[4,513,128]{2,0,1:T(4,128)S(1)} %broadcast_in_dim.65, s32[768]{0:T(1024)S(1)} %fusion.8, f32[768,4,128]{2,1,0:T(4,128)S(1)} %copy.73), kind=kCustom, calls=%fused_computation.4 | custom fusion | flops 393216 | bytes 4721664 | tf_op jit(solution)/shard_map/scatter-add | solution.py:77
  194.1 0.1 slice_bitcast_fusion
  194.1 1.0 copy.74
  (13 shorter events, 0.1 us)
Async XLA Ops:
  20.8 7.0 %all-to-all-start.1 = ((s32[4,1,192]{2,1,0:T(1,128)}), s32[4,1,192]{2,1,0:T(1,128)S(1)}, u32[]{:S(2)}, u32[]{:S(2)}) async-start(s32[4,1,192]{2,1,0:T(1,128)} %reshape.172), calls=%async_computation.1 | async-start | bytes 8192 | tf_op jit(solution)/shard_map/all_to_all | solution.py:32
  56.1 4.7 %copy-start = (f32[512,256]{1,0:T(8,128)S(1)}, f32[512,256]{1,0:T(8,128)}, u32[]{:S(2)}) copy-start(f32[512,256]{1,0:T(8,128)} %param.8) | copy-start | bytes 1572868
  57.3 15.1 %all-to-all-start.3 = ((bf16[4,8,4,24,128]{4,0,3,1,2:T(4,128)(2,1)}), bf16[4,8,4,24,128]{4,0,3,1,2:T(4,128)(2,1)S(1)}, u32[]{:S(2)}, u32[]{:S(2)}) async-start(bf16[4,8,4,24,128]{4,0,3,1,2:T(4,128)(2,1)} %copy.65), calls=%async_computation.3 | async-start | bytes 1572864 | tf_op jit(solution)/shard_map/all_to_all | solution.py:42
  74.8 7.1 %copy-start.2 = (f32[64,64]{1,0:T(8,128)S(1)}, f32[64,64]{1,0:T(8,128)}, u32[]{:S(2)}) copy-start(f32[64,64]{1,0:T(8,128)} %param.9) | copy-start | bytes 49156
  81.9 6.2 %copy-start.1 = (f32[64,64]{1,0:T(8,128)}, f32[64,64]{1,0:T(8,128)S(1)}, u32[]{:S(2)}) copy-start(f32[64,64]{1,0:T(8,128)S(1)} %subtract_select_fusion) | copy-start | bytes 49156
  143.8 23.6 %all-to-all-start.5 = ((f32[4,8,4,24,128]{4,0,3,1,2:T(4,128)}), f32[4,8,4,24,128]{4,0,3,1,2:T(4,128)S(1)}, u32[]{:S(2)}, u32[]{:S(2)}) async-start(f32[4,8,4,24,128]{4,0,3,1,2:T(4,128)} %copy.71), calls=%async_computation.5 | async-start | bytes 3145728 | tf_op jit(solution)/shard_map/all_to_all | solution.py:68
where the time goes:
time: 196 us; the launch traced here: 195 us
  blocking collectives  76.9 us (39%)
  waiting for transfers between devices  32.9 us (17%)
  other arithmetic  31 us (16%)
  local copies, waits for them, and re-layouts  29.8 us (15%)
  matrix products  12.6 us (6%)
  starting transfers between devices  10.3 us (5%)
    all_to_all x1, blocking collectives, per_device(): lax.all_to_all(outgoing, 'lat', split_axis=1, concat_axis=1, tiled=True)  40.5 us
    scatter-add x1, other arithmetic, per_device(): brick_sum.at[:, segment.reshape(-1)]  25.2 us
    all_to_all x1, blocking collectives, per_device(): lax.all_to_all(blocks, 'lat', split_axis=1, concat_axis=1, tiled=True)  22.8 us
    all_to_all x1, waiting for transfers between devices, per_device(): lax.all_to_all(lax.all_to_all(outgoing, 'lat', split_axis=1, concat_axis=...  19.9 us
    scatter x1, local copies, waits for them, and re-layouts, per_device(): outgoing = jnp.zeros((param_count, slot_total, cell_count), jnp.float32)....  13.7 us
    all_to_all x1, blocking collectives, per_device(): lax.all_to_all(wanted, 'lat', split_axis=0, concat_axis=0, tiled=True)  13.6 us
    all_to_all x1, waiting for transfers between devices, per_device(): lax.all_to_all(lax.all_to_all(blocks, 'lat', split_axis=1, concat_axis=1,...  11 us
    dot_general x1, matrix products, per_device(): jnp.einsum('hbc,phc->hpb', kernel, own_blocks, preferred_element_type=jnp...  6.97 us
  transfers between devices with their start and end apart: 3, of which 3 were waited for; matrix products, arithmetic and copies ran while one was open for 1% of the time, Pallas kernels for 0%

commit v1 on v0

v1 whole, which is shorter than its diff:
```python
import functools

import jax
import jax.numpy as jnp
from jax import lax
from jax.experimental import pallas as pl
from jax.experimental.pallas import tpu as pltpu
from jax.sharding import PartitionSpec as P

MESH = pl.DeviceIdType.MESH
F32 = jnp.float32
BF16 = jnp.bfloat16
GROUP = 8
UNROLL = 4


def tomography(
    lat_count,
    dep_count,
    slots,
    target_ref,
    tile_ref,
    count_ref,
    model_ref,
    coefficient_ref,
    observed_ref,
    kernel_hbm,
    residual_ref,
    gradient_ref,
    kernel_vmem,
    model_low,
    request_out,
    request_in,
    request_rows,
    pick,
    pick_t,
    place,
    place_t,
    model_out,
    model_in,
    model_rows,
    own,
    term,
    term_out,
    term_in,
    term_rows,
    kernel_sem,
    request_send,
    request_recv,
    model_send,
    model_recv,
    term_send,
    term_recv,
):
    devices = lat_count * dep_count
    params, tiles, cells = model_ref.shape
    hits = target_ref.shape[1]
    rays, bands = residual_ref.shape
    per_ray = hits // rays
    slot_total = devices * slots
    me = lax.axis_index("lat") * dep_count + lax.axis_index("dep")
    chunks = devices // GROUP
    group_rows = GROUP * slots

    def where_is(device):
        return (device // dep_count, device % dep_count)

    load = pltpu.make_async_copy(kernel_hbm, kernel_vmem, kernel_sem)
    load.start()

    barrier = pltpu.get_barrier_semaphore()

    @pl.loop(1, devices)
    def _(i):
        pl.semaphore_signal(
            barrier, inc=1, device_id=where_is((me + i) % devices), device_id_type=MESH
        )

    target = target_ref[...]
    tile = tile_ref[...]
    hit_lane = lax.broadcasted_iota(jnp.int32, (1, hits), 1)
    live = hit_lane < count_ref[0] * per_ray
    brick = lax.broadcasted_iota(jnp.int32, (devices, hits), 0)
    member = jnp.where((target == brick) & live, 1.0, 0.0).astype(F32)
    earlier = jnp.where(
        lax.broadcasted_iota(jnp.int32, (hits, hits), 0)
        < lax.broadcasted_iota(jnp.int32, (hits, hits), 1),
        1.0,
        0.0,
    ).astype(BF16)
    counted = jnp.dot(member.astype(BF16), earlier, preferred_element_type=F32)
    rank = jnp.sum(member * counted, axis=0, keepdims=True)
    ranked = jnp.where(
        lax.broadcasted_iota(jnp.int32, (128, hits), 0) == rank.astype(jnp.int32), 1.0, 0.0
    ).astype(BF16)
    high = (tile >> 5).astype(F32)
    low = (tile & 31).astype(F32) + 1.0
    dims = (((1,), (1,)), ((), ()))
    wanted = 32.0 * lax.dot_general(
        (member * high).astype(BF16), ranked, dims, preferred_element_type=F32
    ) + lax.dot_general((member * low).astype(BF16), ranked, dims, preferred_element_type=F32)
    for s in range(devices):
        request_out[s] = wanted[s : s + 1, :]

    pl.semaphore_wait(barrier, devices - 1)

    def request_copy(device, source):
        return pltpu.make_async_remote_copy(
            src_ref=request_out.at[device],
            dst_ref=request_in.at[source],
            send_sem=request_send.at[device],
            recv_sem=request_recv.at[source],
            device_id=where_is(device),
            device_id_type=MESH,
        )

    def model_copy(device, source):
        return pltpu.make_async_remote_copy(
            src_ref=model_out.at[device],
            dst_ref=model_in.at[source],
            send_sem=model_send.at[device],
            recv_sem=model_recv.at[source],
            device_id=where_is(device),
            device_id_type=MESH,
        )

    def term_copy(device, source):
        return pltpu.make_async_remote_copy(
            src_ref=term_out.at[device],
            dst_ref=term_in.at[source],
            send_sem=term_send.at[device],
            recv_sem=term_recv.at[source],
            device_id=where_is(device),
            device_id_type=MESH,
        )

    @pl.loop(0, devices)
    def _(i):
        device = (me + devices // 2 + i) % devices

        @pl.when(device != me)
        def _():
            request_copy(device, me).start()

    request_in[me] = request_out[me]

    slot = jnp.where(live, (target * slots).astype(F32) + rank, -1.0)
    for c in range(chunks):
        rows = lax.broadcasted_iota(jnp.int32, (group_rows, hits), 0) + c * group_rows
        place_t[c * group_rows : (c + 1) * group_rows, :] = jnp.where(
            rows.astype(F32) == slot, 1.0, 0.0
        ).astype(BF16)
    slot_column = jnp.transpose(jnp.broadcast_to(slot, (128, hits)))
    lane = lax.broadcasted_iota(jnp.int32, (hits, 128), 1).astype(F32)
    for m in range(slot_total // 128):
        place[:, m * 128 : (m + 1) * 128] = jnp.where(
            lane + float(m * 128) == slot_column, 1.0, 0.0
        ).astype(BF16)
    for p in range(params):
        model_low[:, p * cells : (p + 1) * cells] = model_ref[p].astype(BF16)
    request_rows[...] = jnp.zeros_like(request_rows)

    @pl.loop(1, devices)
    def _(i):
        request_copy((me + i) % devices, (me + i) % devices).wait_recv()

    for d in range(devices):
        request_rows[d : d + 1, :] = request_in[d]
    asked = jnp.transpose(request_rows[...])
    tile_lane = lax.broadcasted_iota(jnp.int32, (slots, tiles), 1).astype(F32) + 1.0
    for d in range(0, devices, 2):
        both = [
            jnp.where(asked[0:slots, e : e + 1] == tile_lane, 1.0, 0.0).astype(F32)
            for e in (d, d + 1)
        ]
        pick[d * slots : (d + 2) * slots, :] = jnp.concatenate(both, axis=0).astype(BF16)

    def send_group(step, matrix, values, out, back, copy):
        chunk = (me // GROUP + chunks // 2 + step) % chunks
        rows = pl.multiple_of(chunk * group_rows, group_rows)
        made = jnp.dot(
            matrix[pl.ds(rows, group_rows), :], values[...], preferred_element_type=F32
        )
        for k in range(GROUP):
            part = made[k * slots : (k + 1) * slots, :]
            block = jnp.concatenate(
                [part[:, p * cells : (p + 1) * cells] for p in range(params)], axis=0
            ).astype(BF16)
            out[chunk * GROUP + k] = block

        @pl.loop(0, GROUP)
        def _(k):
            device = chunk * GROUP + (me + k) % GROUP

            @pl.when(device != me)
            def _():
                copy(device, me).start()

            @pl.when(device == me)
            def _():
                back[me] = out[me]

    @pl.loop(0, chunks)
    def _(step):
        send_group(step, pick, model_low, model_out, model_in, model_copy)

    for m in range(slot_total // 128):
        pick_t[:, m * 128 : (m + 1) * 128] = jnp.transpose(
            pick[m * 128 : (m + 1) * 128, :].astype(F32)
        ).astype(BF16)

    def settle(blocks, rows_ref):
        @pl.loop(0, devices // 2)
        def _(i):
            both = []
            for e in range(2):
                block = blocks[2 * i + e].astype(F32)
                both.append(
                    jnp.concatenate(
                        [block[p * slots : (p + 1) * slots, :] for p in range(params)], axis=1
                    )
                )
            rows = pl.multiple_of(i * 2 * slots, 2 * slots)
            rows_ref[pl.ds(rows, 2 * slots), :] = jnp.concatenate(both, axis=0).astype(BF16)

    @pl.loop(1, devices)
    def _(i):
        model_copy((me + i) % devices, (me + i) % devices).wait_recv()

    settle(model_in, model_rows)

    @pl.loop(0, hits // 128)
    def _(i):
        rows = pl.multiple_of(i * 128, 128)
        own[pl.ds(rows, 128), :] = jnp.dot(
            place[pl.ds(rows, 128), :], model_rows[...], preferred_element_type=F32
        )

    load.wait()

    wide = per_ray * bands
    half = lax.broadcasted_iota(jnp.int32, (per_ray, 2 * bands), 1) < bands
    diagonal = (
        lax.broadcasted_iota(jnp.int32, (per_ray, wide), 1) // bands
        == lax.broadcasted_iota(jnp.int32, (per_ray, wide), 0)
    )

    def one_ray(ray):
        first = pl.multiple_of(ray * per_ray, per_ray)
        block = own[pl.ds(first, per_ray), :]
        block = jnp.concatenate(
            [block[:, p * cells : (p + 1) * cells] for p in range(params)], axis=0
        ).astype(BF16)
        tile_rows = pl.ds(pl.multiple_of(ray * wide, wide), wide)
        tile_block = kernel_vmem[tile_rows, :]
        coefficient = coefficient_ref[pl.ds(first, per_ray), :]
        spread = []
        for p in range(0, params, 2):
            pair = coefficient[:, p * bands : (p + 2) * bands]
            turned = pltpu.roll(pair, bands, 1)
            spread.append(jnp.where(half, pair, turned))
            spread.append(jnp.where(half, turned, pair))
        spread = [
            jnp.where(diagonal, jnp.concatenate([s] * (per_ray // 2), axis=1), 0.0) for s in spread
        ]
        spread = jnp.concatenate(spread, axis=0)
        sensitivity = lax.dot_general(block, tile_block, dims, preferred_element_type=F32)
        predicted = jnp.sum(spread * sensitivity, axis=0, keepdims=True)
        folded = predicted[:, 0 : 2 * bands]
        for k in range(1, per_ray // 2):
            folded = folded + predicted[:, 2 * bands * k : 2 * bands * (k + 1)]
        folded = folded + pltpu.roll(folded, bands, 1)
        observed = observed_ref[pl.ds(ray, 1), :]
        observed = jnp.concatenate([observed, observed], axis=1)
        residual = jnp.where(
            jnp.full(folded.shape, ray, jnp.int32) < count_ref[0], folded - observed, 0.0
        )
        residual_ref[pl.ds(ray, 1), :] = residual[:, 0:bands]
        weight = (spread * jnp.concatenate([residual] * (per_ray // 2), axis=1)).astype(BF16)
        back = jnp.dot(weight, tile_block, preferred_element_type=F32)
        return jnp.concatenate(
            [back[p * per_ray : (p + 1) * per_ray, :] for p in range(params)], axis=1
        )

    @pl.loop(0, rays // UNROLL)
    def _(i):
        made = jnp.concatenate([one_ray(i * UNROLL + u) for u in range(UNROLL)], axis=0)
        count = UNROLL * per_ray
        term[pl.ds(pl.multiple_of(i * count, count), count), :] = made.astype(BF16)

    @pl.loop(0, chunks)
    def _(step):
        send_group(step, place_t, term, term_out, term_in, term_copy)

    @pl.loop(1, devices)
    def _(i):
        device = (me + i) % devices
        request_copy(device, device).wait_send()
        model_copy(device, device).wait_send()

    @pl.loop(1, devices)
    def _(i):
        term_copy((me + i) % devices, (me + i) % devices).wait_recv()

    settle(term_in, term_rows)

    @pl.loop(0, tiles // 128)
    def _(i):
        rows = pl.multiple_of(i * 128, 128)
        summed = jnp.dot(
            pick_t[pl.ds(rows, 128), :], term_rows[...], preferred_element_type=F32
        )
        for p in range(params):
            gradient_ref[p, pl.ds(rows, 128), :] = summed[:, p * cells : (p + 1) * cells]

    @pl.loop(1, devices)
    def _(i):
        device = (me + i) % devices
        term_copy(device, device).wait_send()


def per_device(kernel, coefficient, observed, ray_brick, tile_index, ray_count, earth_model):
    hits, bands, cells = kernel.shape
    _, params, tiles, _ = earth_model.shape
    rays = observed.shape[0]
    lat_count = lax.axis_size("lat")
    dep_count = lax.axis_size("dep")
    devices = lat_count * dep_count
    cap = max(2, 3 * hits // (2 * devices))
    slots = -(-cap // 8) * 8
    total = devices * slots
    wide = params * cells
    vmem = pl.BlockSpec(memory_space=pltpu.VMEM)
    blocks = pltpu.VMEM((devices, params * slots, cells), BF16)
    sems = pltpu.SemaphoreType.DMA((devices,))
    residual, gradient = pl.pallas_call(
        functools.partial(tomography, lat_count, dep_count, slots),
        out_shape=(
            jax.ShapeDtypeStruct((rays, bands), F32),
            jax.ShapeDtypeStruct((params, tiles, cells), F32),
        ),
        in_specs=[
            vmem,
            vmem,
            pl.BlockSpec(memory_space=pltpu.SMEM),
            vmem,
            vmem,
            vmem,
            pl.BlockSpec(memory_space=pl.ANY),
        ],
        out_specs=(vmem, vmem),
        scratch_shapes=[
            pltpu.VMEM((hits * bands, cells), BF16),
            pltpu.VMEM((tiles, wide), BF16),
            pltpu.VMEM((devices, 1, 128), F32),
            pltpu.VMEM((devices, 1, 128), F32),
            pltpu.VMEM((-(-devices // 128) * 128, 128), F32),
            pltpu.VMEM((total, tiles), BF16),
            pltpu.VMEM((tiles, total), BF16),
            pltpu.VMEM((hits, total), BF16),
            pltpu.VMEM((total, hits), BF16),
            blocks,
            blocks,
            pltpu.VMEM((total, wide), BF16),
            pltpu.VMEM((hits, wide), F32),
            pltpu.VMEM((hits, wide), BF16),
            blocks,
            blocks,
            pltpu.VMEM((total, wide), BF16),
            pltpu.SemaphoreType.DMA,
            sems,
            sems,
            sems,
            sems,
            sems,
            sems,
        ],
        compiler_params=pltpu.CompilerParams(
            collective_id=0, has_side_effects=True, vmem_limit_bytes=56 * 1024 * 1024
        ),
        cost_estimate=pl.CostEstimate(
            flops=4 * hits * bands * cells * params, bytes_accessed=hits * bands * cells * 2, transcendentals=0
        ),
        name="tomography",
    )(
        ray_brick.reshape(1, hits),
        tile_index.reshape(1, hits),
        ray_count,
        earth_model[0],
        coefficient,
        observed,
        kernel.reshape(hits * bands, cells),
    )
    return residual, gradient[None]


def solution(mesh):
    return jax.shard_map(
        per_device,
        mesh=mesh,
        in_specs=(
            P(("lat", "dep"), None, None),
            P(("lat", "dep"), None),
            P(("lat", "dep"), None),
            P(("lat", "dep"), None),
            P(("lat", "dep")),
            P(("lat", "dep")),
            P(("lat", "dep"), None, None, None),
        ),
        out_specs=(P(("lat", "dep"), None), P(("lat", "dep"), None, None, None)),
        check_vma=False,
    )
```

time: 196 us -> 75.9 us (0.39)
  blocking collectives: 76.9 us -> 0 us
  Pallas kernels: 0 us -> 70.7 us
  waiting for transfers between devices: 32.9 us -> 0 us
  other arithmetic: 31 us -> 0 us
  local copies, waits for them, and re-layouts: 29.8 us -> 3.64 us
  matrix products: 12.6 us -> 0 us
  starting transfers between devices: 10.3 us -> 0 us
    all_to_all x3 -> x0, blocking collectives: 76.9 us -> none  [the longest x1 40.5 us: per_device(): lax.all_to_all(outgoing, 'lat', split_axis=1, concat_axis=1, tiled=True)]
    pallas_call x0 -> x1, Pallas kernels: none -> 70.7 us  [per_device(): pl.pallas_call(functools.partial(tomography, lat_count, dep_count, slots)...]
    all_to_all x3 -> x0, waiting for transfers between devices: 32.9 us -> none  [the longest x1 19.9 us: per_device(): lax.all_to_all(lax.all_to_all(outgoing, 'lat', split_axis=1, concat_axis=...]
    scatter-add x1 -> x0, other arithmetic: 25.2 us -> none  [per_device(): brick_sum.at[:, segment.reshape(-1)]]
    scatter x2 -> x0, local copies, waits for them, and re-layouts: 16.1 us -> none  [the longest x1 13.7 us: per_device(): outgoing = jnp.zeros((param_count, slot_total, cell_count), jnp.float32)....]
    dot_general x2 -> x0, matrix products: 12.6 us -> none  [the longest x1 6.97 us: per_device(): jnp.einsum('hbc,phc->hpb', kernel, own_blocks, preferred_element_type=jnp...]
    all_to_all x3 -> x0, starting transfers between devices: 10.3 us -> none  [the longest x1 3.56 us: per_device(): lax.all_to_all(lax.all_to_all(outgoing, 'lat', split_axis=1, concat_axis=...]
    gather x2 -> x0, local copies, waits for them, and re-layouts: 4.92 us -> none  [the longest x1 2.84 us: per_device(): blocks = jnp.take(model_low, lookup.reshape(-1), axis=1)]
  transfers between devices with their start and end apart: 3 -> 0, of which waited for: 3 -> 0; matrix products, arithmetic and copies ran while one was open for 1% -> 0% of each run, Pallas kernels for 0% -> 0%
where the time goes in v1:
time: 75.9 us; the launch traced here: 75.6 us
  Pallas kernels  70.7 us (93%)
  local copies, waits for them, and re-layouts  3.64 us (5%)
  between operations  1.29 us (2%)
    pallas_call x1, Pallas kernels, per_device(): pl.pallas_call(functools.partial(tomography, lat_count, dep_count, slots)...  70.7 us
    unnamed x2, local copies, waits for them, and re-layouts  3.64 us

profile of v1, /device:TPU:0, one launch (start us, length us, event | category | flops | bytes accessed | tf_op | source)
XLA Modules:
  0.0 75.6 jit_solution(13762072556120718016)
XLA Ops:
  1.3 70.7 %tomography.1 = (f32[64,64]{1,0:T(8,128)}, f32[4,512,128]{2,1,0:T(8,128)}) custom-call(s32[1,512]{1,0:T(1,128)} %bitcast.8, s32[1,512]{1,0:T(1,128)} %bitcast.9, s32[1]{0:T(128)S(6)} %copy.11.count_ref, f32[4,512,128]{2,1,0:T(8,128)} %bitcast.6, f32[512,256]{1,0:T(8,128)} %coefficient_ref.1, f32[64,64]{1,0:T(8,128)} %observed_ref.1, bf16[32768,128]{1,0:T(8,128)(2,1)} %bitcast.5), custom_call_target="tpu_custom_call" | custom-call | flops 67108864 | bytes 8388608 | tf_op jit(solution)/shard_map/tomography/pallas_call | solution.py:336
  72.0 1.4 %copy.12 = f32[64,64]{1,0:T(8,128)} copy(f32[64,64]{1,0:T(8,128)} %get-tuple-element.8) | data formatting | bytes 32768
  73.3 2.3 %copy.13 = f32[1,4,512,128]{3,2,1,0:T(8,128)} copy(f32[1,4,512,128]{3,2,1,0:T(8,128)} %bitcast.7) | data formatting | bytes 2097152

commit v2 on v1

--- a/solution.py
+++ b/solution.py
@@ -11,7 +11,7 @@
 F32 = jnp.float32
 BF16 = jnp.bfloat16
 GROUP = 8
-UNROLL = 4
+UNROLL = 8
 
 
 def tomography(
@@ -21,13 +21,16 @@
     target_ref,
     tile_ref,
     count_ref,
-    model_ref,
-    coefficient_ref,
-    observed_ref,
+    model_hbm,
+    coefficient_hbm,
+    observed_hbm,
     kernel_hbm,
     residual_ref,
     gradient_ref,
     kernel_vmem,
+    model_ref,
+    coefficient_ref,
+    observed_ref,
     model_low,
     request_out,
     request_in,
@@ -43,8 +46,7 @@
     term,
     term_out,
     term_in,
-    term_rows,
-    kernel_sem,
+    load_sem,
     request_send,
     request_recv,
     model_send,
@@ -58,15 +60,26 @@
     rays, bands = residual_ref.shape
     per_ray = hits // rays
     slot_total = devices * slots
-    me = lax.axis_index("lat") * dep_count + lax.axis_index("dep")
+    me = lax.axis_index("dep") * lat_count + lax.axis_index("lat")
     chunks = devices // GROUP
     group_rows = GROUP * slots
 
     def where_is(device):
-        return (device // dep_count, device % dep_count)
-
-    load = pltpu.make_async_copy(kernel_hbm, kernel_vmem, kernel_sem)
-    load.start()
+        return (device % lat_count, device // lat_count)
+
+    loads = [
+        pltpu.make_async_copy(source, held, load_sem.at[i])
+        for i, (source, held) in enumerate(
+            [
+                (model_hbm, model_ref),
+                (coefficient_hbm, coefficient_ref),
+                (observed_hbm, observed_ref),
+                (kernel_hbm, kernel_vmem),
+            ]
+        )
+    ]
+    for load in loads:
+        load.start()
 
     barrier = pltpu.get_barrier_semaphore()
 
@@ -77,6 +90,7 @@
         )
 
     target = target_ref[...]
+    target = (target % dep_count) * lat_count + target // dep_count
     tile = tile_ref[...]
     hit_lane = lax.broadcasted_iota(jnp.int32, (1, hits), 1)
     live = hit_lane < count_ref[0] * per_ray
@@ -150,12 +164,7 @@
         place_t[c * group_rows : (c + 1) * group_rows, :] = jnp.where(
             rows.astype(F32) == slot, 1.0, 0.0
         ).astype(BF16)
-    slot_column = jnp.transpose(jnp.broadcast_to(slot, (128, hits)))
-    lane = lax.broadcasted_iota(jnp.int32, (hits, 128), 1).astype(F32)
-    for m in range(slot_total // 128):
-        place[:, m * 128 : (m + 1) * 128] = jnp.where(
-            lane + float(m * 128) == slot_column, 1.0, 0.0
-        ).astype(BF16)
+    loads[0].wait()
     for p in range(params):
         model_low[:, p * cells : (p + 1) * cells] = model_ref[p].astype(BF16)
     request_rows[...] = jnp.zeros_like(request_rows)
@@ -190,7 +199,8 @@
 
         @pl.loop(0, GROUP)
         def _(k):
-            device = chunk * GROUP + (me + k) % GROUP
+            turn = 4 * ((k + 1) % 2) + 2 * ((k // 2) % 2) + k // 4
+            device = chunk * GROUP + (me + turn) % GROUP
 
             @pl.when(device != me)
             def _():
@@ -204,39 +214,56 @@
     def _(step):
         send_group(step, pick, model_low, model_out, model_in, model_copy)
 
-    for m in range(slot_total // 128):
-        pick_t[:, m * 128 : (m + 1) * 128] = jnp.transpose(
-            pick[m * 128 : (m + 1) * 128, :].astype(F32)
+    slot_column = jnp.transpose(jnp.broadcast_to(slot, (256, hits)))[:, 0:group_rows]
+    lane = lax.broadcasted_iota(jnp.int32, (hits, group_rows), 1).astype(F32)
+    for c in range(chunks):
+        place[c] = jnp.where(lane + float(c * group_rows) == slot_column, 1.0, 0.0).astype(BF16)
+        pick_t[c] = jnp.transpose(
+            pick[c * group_rows : (c + 1) * group_rows, :].astype(F32)
         ).astype(BF16)
-
-    def settle(blocks, rows_ref):
-        @pl.loop(0, devices // 2)
-        def _(i):
+    own[...] = jnp.zeros_like(own)
+
+    def take_group(step, matrix, blocks, rows_ref, copy, add):
+        chunk = (me // GROUP + chunks // 2 - step + chunks) % chunks
+
+        @pl.loop(0, GROUP)
+        def _(k):
+            device = chunk * GROUP + k
+
+            @pl.when(device != me)
+            def _():
+                copy(device, device).wait_recv()
+
+        for k in range(0, GROUP, 2):
             both = []
             for e in range(2):
-                block = blocks[2 * i + e].astype(F32)
+                block = blocks[chunk * GROUP + k + e].astype(F32)
                 both.append(
                     jnp.concatenate(
                         [block[p * slots : (p + 1) * slots, :] for p in range(params)], axis=1
                     )
                 )
-            rows = pl.multiple_of(i * 2 * slots, 2 * slots)
-            rows_ref[pl.ds(rows, 2 * slots), :] = jnp.concatenate(both, axis=0).astype(BF16)
-
-    @pl.loop(1, devices)
-    def _(i):
-        model_copy((me + i) % devices, (me + i) % devices).wait_recv()
-
-    settle(model_in, model_rows)
-
-    @pl.loop(0, hits // 128)
-    def _(i):
-        rows = pl.multiple_of(i * 128, 128)
-        own[pl.ds(rows, 128), :] = jnp.dot(
-            place[pl.ds(rows, 128), :], model_rows[...], preferred_element_type=F32
-        )
-
-    load.wait()
+            rows_ref[k * slots : (k + 2) * slots, :] = jnp.concatenate(both, axis=0).astype(BF16)
+
+        @pl.loop(0, matrix.shape[1] // 128)
+        def _(i):
+            rows = pl.multiple_of(i * 128, 128)
+            add(
+                rows,
+                jnp.dot(
+                    matrix[chunk, pl.ds(rows, 128), :], rows_ref[...], preferred_element_type=F32
+                ),
+            )
+
+    def add_own(rows, part):
+        own[pl.ds(rows, 128), :] += part
+
+    @pl.loop(0, chunks)
+    def _(step):
+        take_group(step, place, model_in, model_rows, model_copy, add_own)
+
+    for load in loads[1:]:
+        load.wait()
 
     wide = per_ray * bands
     half = lax.broadcasted_iota(jnp.int32, (per_ray, 2 * bands), 1) < bands
@@ -298,20 +325,15 @@
         request_copy(device, device).wait_send()
         model_copy(device, device).wait_send()
 
-    @pl.loop(1, devices)
-    def _(i):
-        term_copy((me + i) % devices, (me + i) % devices).wait_recv()
-
-    settle(term_in, term_rows)
-
-    @pl.loop(0, tiles // 128)
-    def _(i):
-        rows = pl.multiple_of(i * 128, 128)
-        summed = jnp.dot(
-            pick_t[pl.ds(rows, 128), :], term_rows[...], preferred_element_type=F32
-        )
+    gradient_ref[...] = jnp.zeros_like(gradient_ref)
+
+    def add_gradient(rows, part):
         for p in range(params):
-            gradient_ref[p, pl.ds(rows, 128), :] = summed[:, p * cells : (p + 1) * cells]
+            gradient_ref[p, pl.ds(rows, 128), :] += part[:, p * cells : (p + 1) * cells]
+
+    @pl.loop(0, chunks)
+    def _(step):
+        take_group(step, pick_t, term_in, model_rows, term_copy, add_gradient)
 
     @pl.loop(1, devices)
     def _(i):
@@ -343,31 +365,30 @@
             vmem,
             vmem,
             pl.BlockSpec(memory_space=pltpu.SMEM),
-            vmem,
-            vmem,
-            vmem,
-            pl.BlockSpec(memory_space=pl.ANY),
-        ],
+        ]
+        + [pl.BlockSpec(memory_space=pl.ANY)] * 4,
         out_specs=(vmem, vmem),
         scratch_shapes=[
             pltpu.VMEM((hits * bands, cells), BF16),
+            pltpu.VMEM((params, tiles, cells), F32),
+            pltpu.VMEM((hits, params * bands), F32),
+            pltpu.VMEM((rays, bands), F32),
             pltpu.VMEM((tiles, wide), BF16),
             pltpu.VMEM((devices, 1, 128), F32),
             pltpu.VMEM((devices, 1, 128), F32),
             pltpu.VMEM((-(-devices // 128) * 128, 128), F32),
             pltpu.VMEM((total, tiles), BF16),
-            pltpu.VMEM((tiles, total), BF16),
-            pltpu.VMEM((hits, total), BF16),
+            pltpu.VMEM((devices // GROUP, tiles, GROUP * slots), BF16),
+            pltpu.VMEM((devices // GROUP, hits, GROUP * slots), BF16),
             pltpu.VMEM((total, hits), BF16),
             blocks,
             blocks,
-            pltpu.VMEM((total, wide), BF16),
+            pltpu.VMEM((GROUP * slots, wide), BF16),
             pltpu.VMEM((hits, wide), F32),
             pltpu.VMEM((hits, wide), BF16),
             blocks,
             blocks,
-            pltpu.VMEM((total, wide), BF16),
-            pltpu.SemaphoreType.DMA,
+            pltpu.SemaphoreType.DMA((4,)),
             sems,
             sems,
             sems,

time: 75.9 us -> 76.7 us (1.011)
  Pallas kernels: 70.7 us -> 71.5 us
    pallas_call x1, Pallas kernels: 70.7 us -> 71.5 us  [per_device(): pl.pallas_call(functools.partial(tomography, lat_count, dep_count, slots)...]
where the time goes in v2:
time: 76.7 us; the launch traced here: 76.4 us
  Pallas kernels  71.5 us (93%)
  local copies, waits for them, and re-layouts  3.64 us (5%)
  between operations  1.29 us (2%)
    pallas_call x1, Pallas kernels, per_device(): pl.pallas_call(functools.partial(tomography, lat_count, dep_count, slots)...  71.5 us
    unnamed x2, local copies, waits for them, and re-layouts  3.64 us

profile of v2, /device:TPU:0, one launch (start us, length us, event | category | flops | bytes accessed | tf_op | source)
XLA Modules:
  0.0 76.4 jit_solution(18129424351208552307)
XLA Ops:
  1.3 71.5 %tomography.1 = (f32[64,64]{1,0:T(8,128)}, f32[4,512,128]{2,1,0:T(8,128)}) custom-call(s32[1,512]{1,0:T(1,128)} %bitcast.8, s32[1,512]{1,0:T(1,128)} %bitcast.9, s32[1]{0:T(128)S(6)} %copy.11.count_ref, f32[4,512,128]{2,1,0:T(8,128)} %bitcast.6, f32[512,256]{1,0:T(8,128)} %coefficient_hbm.1, f32[64,64]{1,0:T(8,128)} %observed_hbm.1, bf16[32768,128]{1,0:T(8,128)(2,1)} %bitcast.5), custom_call_target="tpu_custom_call" | custom-call | flops 67108864 | bytes 8388608 | tf_op jit(solution)/shard_map/tomography/pallas_call | solution.py:358
  72.8 1.4 %copy.12 = f32[64,64]{1,0:T(8,128)} copy(f32[64,64]{1,0:T(8,128)} %get-tuple-element.8) | data formatting | bytes 32768
  74.2 2.3 %copy.13 = f32[1,4,512,128]{3,2,1,0:T(8,128)} copy(f32[1,4,512,128]{3,2,1,0:T(8,128)} %bitcast.7) | data formatting | bytes 2097152
